TPU v7x, 32 devices: a whole 2x2x4 slice. The times are simulated.
32 devices in a mesh: seg: 16 (over z, y, x), samp: 2 (over core).
Axes of the slice: x: 2, y: 2, z: 4, core: 2. Of those that a mesh axis runs over, the one named last changes fastest.
Arguments:
- rigidity_diagonal_cells: bfloat16 [512, 128, 128], P('seg')
- rigidity_lower_cells: bfloat16 [512, 128, 128], P('seg'), may hold values from -0.5 to 0.5
- inverse_diagonal_cells: bfloat16 [512, 128, 128], P('seg')
- bedding_rigidity_per_unknown: float32 [512, 128], P('seg'), may hold values from 0.3 to 2
- bedding_regime: int32 [512], P('seg'), may hold values from 0 to 2
- dilation_push_per_kelvin: float32 [512, 128], P('seg'), may hold values from 1 to 16
- heat_shape_functions: bfloat16 [512, 512], P('seg'), may hold values from -0.25 to 0.25
- sampled_shape_weights: bfloat16 [64, 512], P('samp'), may hold values from -6 to 6
- joined_segment_table: int32 [16, 2], P('seg'), may hold values from 0 to 15
- joint_rigidity: float32 [16, 2], P('seg'), may hold values from 1.2 to 3.6
Outputs:
- displacement: float32 [64, 512, 128], P('samp', 'seg')
- kl_grad: float32 [512], replicated
Inputs may be any that keep to these rules, and one draw needn't show every extreme that they name: `joined_segment_table`: every entry names a segment.
All inputs are finite; a program needn't handle non-finite values.
Results may differ from a plain program's by a relative error of at most 0.013.
Values may be sent and summed in bfloat16 or wider, within the bound.
A program may use at most 64 MiB of HBM per device.

v0:
```python
import math
import jax
import jax.numpy as jnp
from jax import lax
from jax.sharding import PartitionSpec as P

STEPS = 4


def shifted(value, axis, steps):
    count = lax.axis_size(axis)
    first, last = (max(0, -steps), min(count, count - steps))
    return lax.ppermute(value, axis, [(source, source + steps) for source in range(first, last)])


def stiffness(
    field_round, rigidity_diagonal_cells, rigidity_lower_cells, joined_segment_table, joint_rigidity
):
    own_term = jnp.einsum(
        "sjb,jab->sja", field_round, rigidity_diagonal_cells, preferred_element_type=jnp.float32
    )
    upward = jnp.einsum(
        "sjb,jba->sja", field_round, rigidity_lower_cells, preferred_element_type=jnp.float32
    ).astype(jnp.bfloat16)
    below_rim = shifted(field_round[:, -1:, :], "seg", 1)
    above_rim = shifted(upward[:, :1, :], "seg", -1)
    interfaces = lax.all_gather(field_round[:, :1, :], "seg", axis=1, tiled=True)
    lower_field = jnp.concatenate([below_rim, field_round[:, :-1]], axis=1)
    below_term = jnp.einsum(
        "sjb,jab->sja", lower_field, rigidity_lower_cells, preferred_element_type=jnp.float32
    )
    upper_term = jnp.concatenate([upward[:, 1:], above_rim], axis=1).astype(jnp.float32)
    result = own_term + below_term + upper_term
    partner = jnp.take(interfaces, joined_segment_table[0], axis=1).astype(jnp.float32)
    own_interface = field_round[:, 0:1, :].astype(jnp.float32)
    spring = jnp.sum(joint_rigidity[0][None, :, None] * (own_interface - partner), axis=1)
    return result.at[:, 0, :].add(spring)


def ballast(state, bedding_rigidity_per_unknown, bedding_regime):
    code = bedding_regime[None, :, None]
    stiff = bedding_rigidity_per_unknown[None]
    magnitude = 1.0 + jnp.abs(state)
    slide = jnp.tanh(state)
    force = jnp.where(
        code == 0, stiff * state, jnp.where(code == 1, stiff * state / magnitude, stiff * slide)
    )
    tangent = jnp.where(
        code == 0,
        stiff + 0.0 * state,
        jnp.where(code == 1, stiff / (magnitude * magnitude), stiff * (1.0 - slide * slide)),
    )
    return (force, tangent)


def blockwise(inverse_diagonal_cells, field_round):
    return jnp.einsum(
        "jab,sjb->sja", inverse_diagonal_cells, field_round, preferred_element_type=jnp.float32
    )


def body(
    rigidity_diagonal_cells,
    rigidity_lower_cells,
    inverse_diagonal_cells,
    bedding_rigidity_per_unknown,
    bedding_regime,
    dilation_push_per_kelvin,
    heat_shape_functions,
    sampled_shape_weights,
    joined_segment_table,
    joint_rigidity,
):
    samples_here = sampled_shape_weights.shape[0]
    blocks_here = rigidity_diagonal_cells.shape[0]
    width = rigidity_diagonal_cells.shape[1]
    shape_functions = heat_shape_functions.shape[1]
    complete_shape_functions = heat_shape_functions.astype(jnp.float32)
    heat_distribution = jnp.dot(
        sampled_shape_weights, heat_shape_functions.T, preferred_element_type=jnp.float32
    )
    heat_driven_source = dilation_push_per_kelvin[None] * heat_distribution[:, :, None]
    state = jnp.zeros((samples_here, blocks_here, width), jnp.float32)
    grad_total = jnp.zeros((shape_functions,), jnp.float32)
    for iteration in range(STEPS):
        state_round = state.astype(jnp.bfloat16)
        force, tangent = ballast(state, bedding_rigidity_per_unknown, bedding_regime)
        residual_vector = (
            heat_driven_source
            - stiffness(
                state_round,
                rigidity_diagonal_cells,
                rigidity_lower_cells,
                joined_segment_table,
                joint_rigidity,
            )
            - force
        )
        initial_newton_step = blockwise(
            inverse_diagonal_cells, residual_vector.astype(jnp.bfloat16)
        )
        second = (
            residual_vector
            - stiffness(
                initial_newton_step.astype(jnp.bfloat16),
                rigidity_diagonal_cells,
                rigidity_lower_cells,
                joined_segment_table,
                joint_rigidity,
            )
            - tangent * initial_newton_step
        )
        state = (
            state
            + initial_newton_step
            + blockwise(inverse_diagonal_cells, second.astype(jnp.bfloat16))
        )
        adjoint = jnp.einsum(
            "sja,jab->sjb",
            state.astype(jnp.bfloat16),
            inverse_diagonal_cells,
            preferred_element_type=jnp.float32,
        )
        weighted = jnp.sum(jnp.sum(dilation_push_per_kelvin[None] * adjoint, axis=2), axis=0)
        partial_value = jnp.dot(weighted, complete_shape_functions, precision=lax.Precision.HIGHEST)
        grad_total = grad_total + lax.psum(partial_value, ("seg", "samp"))
    every_block_list = blocks_here * lax.axis_size("seg")
    all_samples = samples_here * lax.axis_size("samp")
    scale = math.sqrt(shape_functions / (every_block_list * all_samples * width))
    return (state, grad_total * scale)


def solution(mesh):
    placed = (
        P("seg", None, None),
        P("seg", None, None),
        P("seg", None, None),
        P("seg", None),
        P("seg"),
        P("seg", None),
        P("seg", None),
        P("samp", None),
        P("seg", None),
        P("seg", None),
    )
    return jax.shard_map(
        body, mesh=mesh, in_specs=placed, out_specs=(P("samp", "seg", None), P()), check_vma=False
    )
```

profile of v0, /device:TPU:14, one launch (start us, length us, event | category | flops | bytes accessed | tf_op | source)
XLA Modules:
  0.0 460.8 jit_solution(1154479130879753834)
XLA Ops:
  0.7 3.5 collective-permute-start
  4.6 2.6 collective-permute-start.1
  8.5 1.5 fusion.94
  16.1 1.5 fusion.140
  17.6 4.8 %collective-permute-start.2 = (bf16[32,1,128]{2,0,1:T(8,128)(2,1)}, bf16[32,1,128]{2,0,1:T(8,128)(2,1)}, u32[]{:S(2)}, u32[]{:S(2)}) collective-permute-start(bf16[32,1,128]{2,0,1:T(8,128)(2,1)} %get-tuple-element.125), channel_id=1, source_target_pairs={{0,2},{2,4},{4,6},{6,8},{8,10},{10,12},{12,14},{14,16},{16,18},{18... | collective-permute-start | bytes 24584 | tf_op jit(solution)/shard_map/ppermute | solution.py:13
  22.4 30.9 %all_gather.22 = bf16[32,16,128]{2,0,1:T(8,128)(2,1)} all-gather(bf16[32,1,128]{2,0,1:T(8,128)(2,1)S(1)} %get-tuple-element.124), channel_id=1, replica_groups=mesh['seg'=16,'samp'=2] {'seg'}, dimensions={1}, use_global_device_ids=true | all-gather | bytes 139264 | tf_op jit(solution)/shard_map/all_gather | solution.py:27
  53.3 1.5 gather_fusion.1
  55.5 3.5 collective-permute-start.3
  59.1 4.1 collective-permute-done.3
  64.6 1.5 fusion.133
  68.3 1.5 fusion.141
  69.9 3.9 collective-permute-start.4
  73.8 34.6 %all_gather.23 = bf16[32,16,128]{2,0,1:T(8,128)(2,1)} all-gather(bf16[32,1,128]{2,0,1:T(8,128)(2,1)S(1)} %get-tuple-element.121), channel_id=1, replica_groups=mesh['seg'=16,'samp'=2] {'seg'}, dimensions={1}, use_global_device_ids=true | all-gather | bytes 139264 | tf_op jit(solution)/shard_map/all_gather | solution.py:27
  108.4 1.5 gather_fusion.2
  110.5 1.9 collective-permute-start.5
  112.6 5.3 %collective-permute-done.5 = bf16[32,1,128]{2,0,1:T(8,128)(2,1)S(1)} collective-permute-done((bf16[32,1,128]{2,0,1:T(8,128)(2,1)S(1)}, bf16[32,1,128]{2,0,1:T(8,128)(2,1)S(1)}, u32[]{:S(2)}, u32[]{:S(2)}) %collective-permute-start.5) | collective-permute-done | bytes 8224 | tf_op jit(solution)/shard_map/ppermute | solution.py:13
  119.9 1.5 fusion.134
  124.6 1.9 collective-permute-start.6
  126.5 40.1 %all_gather.24 = bf16[32,16,128]{2,0,1:T(8,128)(2,1)} all-gather(bf16[32,1,128]{2,0,1:T(8,128)(2,1)S(1)} %get-tuple-element.118), channel_id=1, replica_groups=mesh['seg'=16,'samp'=2] {'seg'}, dimensions={1}, use_global_device_ids=true | all-gather | bytes 139264 | tf_op jit(solution)/shard_map/all_gather | solution.py:27
  166.6 1.5 gather_fusion.3
  168.8 1.9 collective-permute-start.7
  170.9 5.2 %collective-permute-done.7 = bf16[32,1,128]{2,0,1:T(8,128)(2,1)S(1)} collective-permute-done((bf16[32,1,128]{2,0,1:T(8,128)(2,1)S(1)}, bf16[32,1,128]{2,0,1:T(8,128)(2,1)S(1)}, u32[]{:S(2)}, u32[]{:S(2)}) %collective-permute-start.7) | collective-permute-done | bytes 8224 | tf_op jit(solution)/shard_map/ppermute | solution.py:13
  178.2 1.6 fusion.135
  181.9 1.5 fusion.143
  184.1 1.9 collective-permute-start.8
  186.0 40.2 %all_gather.25 = bf16[32,16,128]{2,0,1:T(8,128)(2,1)} all-gather(bf16[32,1,128]{2,0,1:T(8,128)(2,1)S(1)} %get-tuple-element.115), channel_id=1, replica_groups=mesh['seg'=16,'samp'=2] {'seg'}, dimensions={1}, use_global_device_ids=true | all-gather | bytes 139264 | tf_op jit(solution)/shard_map/all_gather | solution.py:27
  226.3 1.5 gather_fusion.4
  228.4 1.9 collective-permute-start.9
  230.5 5.3 %collective-permute-done.9 = bf16[32,1,128]{2,0,1:T(8,128)(2,1)S(1)} collective-permute-done((bf16[32,1,128]{2,0,1:T(8,128)(2,1)S(1)}, bf16[32,1,128]{2,0,1:T(8,128)(2,1)S(1)}, u32[]{:S(2)}, u32[]{:S(2)}) %collective-permute-start.9) | collective-permute-done | bytes 8224 | tf_op jit(solution)/shard_map/ppermute | solution.py:13
  237.8 1.5 fusion.136
  242.5 1.9 collective-permute-start.10
  244.4 40.1 %all_gather.26 = bf16[32,16,128]{2,0,1:T(8,128)(2,1)} all-gather(bf16[32,1,128]{2,0,1:T(8,128)(2,1)S(1)} %get-tuple-element.112), channel_id=1, replica_groups=mesh['seg'=16,'samp'=2] {'seg'}, dimensions={1}, use_global_device_ids=true | all-gather | bytes 139264 | tf_op jit(solution)/shard_map/all_gather | solution.py:27
  284.5 1.5 gather_fusion.5
  286.6 2.1 collective-permute-start.11
  288.9 5.0 %collective-permute-done.11 = bf16[32,1,128]{2,0,1:T(8,128)(2,1)S(1)} collective-permute-done((bf16[32,1,128]{2,0,1:T(8,128)(2,1)S(1)}, bf16[32,1,128]{2,0,1:T(8,128)(2,1)S(1)}, u32[]{:S(2)}, u32[]{:S(2)}) %collective-permute-start.11) | collective-permute-done | bytes 8224 | tf_op jit(solution)/shard_map/ppermute | solution.py:13
  296.0 1.6 fusion.137
  299.8 1.5 fusion.145
  301.9 1.9 collective-permute-start.12
  303.9 40.1 %all_gather.27 = bf16[32,16,128]{2,0,1:T(8,128)(2,1)} all-gather(bf16[32,1,128]{2,0,1:T(8,128)(2,1)S(1)} %get-tuple-element.109), channel_id=1, replica_groups=mesh['seg'=16,'samp'=2] {'seg'}, dimensions={1}, use_global_device_ids=true | all-gather | bytes 139264 | tf_op jit(solution)/shard_map/all_gather | solution.py:27
  344.0 1.5 gather_fusion.6
  346.1 2.0 collective-permute-start.13
  348.2 5.2 %collective-permute-done.13 = bf16[32,1,128]{2,0,1:T(8,128)(2,1)S(1)} collective-permute-done((bf16[32,1,128]{2,0,1:T(8,128)(2,1)S(1)}, bf16[32,1,128]{2,0,1:T(8,128)(2,1)S(1)}, u32[]{:S(2)}, u32[]{:S(2)}) %collective-permute-start.13) | collective-permute-done | bytes 8224 | tf_op jit(solution)/shard_map/ppermute | solution.py:13
  355.5 1.5 fusion.138
  359.6 1.9 collective-permute-start.14
  361.5 37.3 %all_gather.28 = bf16[32,16,128]{2,0,1:T(8,128)(2,1)S(1)} all-gather(bf16[32,1,128]{2,0,1:T(8,128)(2,1)S(1)} %get-tuple-element.106), channel_id=1, replica_groups=mesh['seg'=16,'samp'=2] {'seg'}, dimensions={1}, use_global_device_ids=true | all-gather | bytes 139264 | tf_op jit(solution)/shard_map/all_gather | solution.py:27
  400.1 2.0 collective-permute-start.15
  402.2 5.2 %collective-permute-done.15 = bf16[32,1,128]{2,0,1:T(8,128)(2,1)S(1)} collective-permute-done((bf16[32,1,128]{2,0,1:T(8,128)(2,1)S(1)}, bf16[32,1,128]{2,0,1:T(8,128)(2,1)S(1)}, u32[]{:S(2)}, u32[]{:S(2)}) %collective-permute-start.15) | collective-permute-done | bytes 8224 | tf_op jit(solution)/shard_map/ppermute | solution.py:13
  412.1 48.0 %psum.34 = f32[512]{0:T(512)S(1)} all-reduce(f32[512]{0:T(512)S(1)} %add_add_fusion), channel_id=1, replica_groups=mesh['seg'=16,'samp'=2] {'seg','samp'}, use_global_device_ids=true, to_apply=%region_9.11 | all-reduce | flops 512 | bytes 4096 | tf_op jit(solution)/shard_map/psum | solution.py:126
  (210 shorter events, 47.5 us)
Async XLA Ops:
  0.6 7.8 %copy-start.1 = (bf16[32,128,128]{2,1,0:T(8,128)(2,1)S(1)}, bf16[32,128,128]{2,1,0:T(8,128)(2,1)}, u32[]{:S(2)}) copy-start(bf16[32,128,128]{2,1,0:T(8,128)(2,1)} %param.28) | copy-start | bytes 3145732
  0.7 10.2 %collective-permute-start = (bf16[32,1,128]{2,0,1:T(8,128)(2,1)S(1)}, bf16[32,1,128]{2,0,1:T(8,128)(2,1)S(1)}, u32[]{:S(2)}, u32[]{:S(2)}) collective-permute-start(bf16[32,1,128]{2,0,1:T(8,128)(2,1)S(1)} %slice.302), channel_id=1, source_target_pairs={{0,2},{2,4},{4,6},{6,8},{8,10},{10,12},{12,14},{14,16},{16,18},{18... | collective-permute-start | bytes 24584 | tf_op jit(solution)/shard_map/ppermute | solution.py:13
  4.6 3.9 copy-start.26
  4.6 7.5 %collective-permute-start.1 = (bf16[32,1,128]{2,0,1:T(8,128)(2,1)S(1)}, bf16[32,1,128]{2,0,1:T(8,128)(2,1)S(1)}, u32[]{:S(2)}, u32[]{:S(2)}) collective-permute-start(bf16[32,1,128]{2,0,1:T(8,128)(2,1)S(1)} %slice.366), channel_id=1, source_target_pairs={{2,0},{4,2},{6,4},{8,6},{10,8},{12,10},{14,12},{16,14},{18,16},{20... | collective-permute-start | bytes 24584 | tf_op jit(solution)/shard_map/ppermute | solution.py:13
  14.3 44.7 %copy-start.7 = (bf16[32,32,128]{2,0,1:T(8,128)(2,1)}, bf16[32,32,128]{2,0,1:T(8,128)(2,1)S(1)}, u32[]{:S(2)}) copy-start(bf16[32,32,128]{2,0,1:T(8,128)(2,1)S(1)} %convert_bitcast_fusion) | copy-start | bytes 786436
  17.6 41.5 %collective-permute-start.2 = (bf16[32,1,128]{2,0,1:T(8,128)(2,1)}, bf16[32,1,128]{2,0,1:T(8,128)(2,1)}, u32[]{:S(2)}, u32[]{:S(2)}) collective-permute-start(bf16[32,1,128]{2,0,1:T(8,128)(2,1)} %get-tuple-element.125), channel_id=1, source_target_pairs={{0,2},{2,4},{4,6},{6,8},{8,10},{10,12},{12,14},{14,16},{16,18},{18... | collective-permute-start | bytes 24584 | tf_op jit(solution)/shard_map/ppermute | solution.py:13
  55.5 7.7 %collective-permute-start.3 = (bf16[32,1,128]{2,0,1:T(8,128)(2,1)S(1)}, bf16[32,1,128]{2,0,1:T(8,128)(2,1)S(1)}, u32[]{:S(2)}, u32[]{:S(2)}) collective-permute-start(bf16[32,1,128]{2,0,1:T(8,128)(2,1)S(1)} %slice.371), channel_id=1, source_target_pairs={{2,0},{4,2},{6,4},{8,6},{10,8},{12,10},{14,12},{16,14},{18,16},{20... | collective-permute-start | bytes 24584 | tf_op jit(solution)/shard_map/ppermute | solution.py:13
  59.0 4.2 copy-start.13
  59.1 4.1 slice-start
  59.1 4.1 slice-start.5
  59.1 5.5 %copy-start.4 = (f32[32,32,128]{2,0,1:T(8,128)S(1)}, f32[32,32,128]{2,0,1:T(8,128)}, u32[]{:S(2)}) copy-start(f32[32,32,128]{2,0,1:T(8,128)} %copy-done.3) | copy-start | bytes 1572868
  59.1 5.5 %copy-start.6 = (f32[32,32,128]{2,1,0:T(8,128)S(1)}, f32[32,32,128]{2,1,0:T(8,128)}, u32[]{:S(2)}) copy-start(f32[32,32,128]{2,1,0:T(8,128)} %copy-done.5) | copy-start | bytes 1572868
  69.9 42.7 %collective-permute-start.4 = (bf16[32,1,128]{2,0,1:T(8,128)(2,1)}, bf16[32,1,128]{2,0,1:T(8,128)(2,1)}, u32[]{:S(2)}, u32[]{:S(2)}) collective-permute-start(bf16[32,1,128]{2,0,1:T(8,128)(2,1)} %get-tuple-element.122), channel_id=1, source_target_pairs={{0,2},{2,4},{4,6},{6,8},{8,10},{10,12},{12,14},{14,16},{16,18},{18... | collective-permute-start | bytes 24584 | tf_op jit(solution)/shard_map/ppermute | solution.py:13
  110.5 7.3 %collective-permute-start.5 = (bf16[32,1,128]{2,0,1:T(8,128)(2,1)S(1)}, bf16[32,1,128]{2,0,1:T(8,128)(2,1)S(1)}, u32[]{:S(2)}, u32[]{:S(2)}) collective-permute-start(bf16[32,1,128]{2,0,1:T(8,128)(2,1)S(1)} %slice.377), channel_id=1, source_target_pairs={{2,0},{4,2},{6,4},{8,6},{10,8},{12,10},{14,12},{16,14},{18,16},{20... | collective-permute-start | bytes 24584 | tf_op jit(solution)/shard_map/ppermute | solution.py:13
  112.4 5.4 %copy-start.9 = (f32[32,32,128]{2,1,0:T(8,128)S(1)}, f32[32,32,128]{2,1,0:T(8,128)}, u32[]{:S(2)}) copy-start(f32[32,32,128]{2,1,0:T(8,128)} %fusion.141) | copy-start | bytes 1572868
  112.6 5.3 %slice-start.1 = ((bf16[32,32,128]{2,0,1:T(8,128)(2,1)}), bf16[32,31,128]{2,0,1:T(8,128)(2,1)S(1)}, s32[]{:S(2)}) async-start(bf16[32,32,128]{2,0,1:T(8,128)(2,1)} %fusion.26), calls=%async_computation.1 | async-start | bytes 507904 | tf_op jit(solution)/shard_map/slice | solution.py:32
  112.6 6.7 %copy-start.24 = (f32[32,32,128]{2,0,1:T(8,128)S(1)}, f32[32,32,128]{2,0,1:T(8,128)}, u32[]{:S(2)}) copy-start(f32[32,32,128]{2,0,1:T(8,128)} %get-tuple-element.129) | copy-start | bytes 1572868
  124.6 46.3 %collective-permute-start.6 = (bf16[32,1,128]{2,0,1:T(8,128)(2,1)}, bf16[32,1,128]{2,0,1:T(8,128)(2,1)}, u32[]{:S(2)}, u32[]{:S(2)}) collective-permute-start(bf16[32,1,128]{2,0,1:T(8,128)(2,1)} %get-tuple-element.119), channel_id=1, source_target_pairs={{0,2},{2,4},{4,6},{6,8},{8,10},{10,12},{12,14},{14,16},{16,18},{18... | collective-permute-start | bytes 24584 | tf_op jit(solution)/shard_map/ppermute | solution.py:13
  168.8 7.3 %collective-permute-start.7 = (bf16[32,1,128]{2,0,1:T(8,128)(2,1)S(1)}, bf16[32,1,128]{2,0,1:T(8,128)(2,1)S(1)}, u32[]{:S(2)}, u32[]{:S(2)}) collective-permute-start(bf16[32,1,128]{2,0,1:T(8,128)(2,1)S(1)} %slice.383), channel_id=1, source_target_pairs={{2,0},{4,2},{6,4},{8,6},{10,8},{12,10},{14,12},{16,14},{18,16},{20... | collective-permute-start | bytes 24584 | tf_op jit(solution)/shard_map/ppermute | solution.py:13
  170.7 5.4 %copy-start.14 = (f32[32,32,128]{2,1,0:T(8,128)S(1)}, f32[32,32,128]{2,1,0:T(8,128)}, u32[]{:S(2)}) copy-start(f32[32,32,128]{2,1,0:T(8,128)} %fusion.142) | copy-start | bytes 1572868
  170.8 5.3 %slice-start.6 = ((bf16[32,32,128]{2,0,1:T(8,128)(2,1)}), bf16[32,31,128]{2,0,1:T(8,128)(2,1)S(1)}, s32[]{:S(2)}) async-start(bf16[32,32,128]{2,0,1:T(8,128)(2,1)} %fusion.27), calls=%async_computation.6 | async-start | bytes 507904 | tf_op jit(solution)/shard_map/slice | solution.py:32
  170.8 6.7 %copy-start.19 = (f32[32,32,128]{2,0,1:T(8,128)S(1)}, f32[32,32,128]{2,0,1:T(8,128)}, u32[]{:S(2)}) copy-start(f32[32,32,128]{2,0,1:T(8,128)} %copy-done.18) | copy-start | bytes 1572868
  170.9 6.7 %copy-start.25 = (f32[32,32,128]{2,0,1:T(8,128)S(1)}, f32[32,32,128]{2,0,1:T(8,128)}, u32[]{:S(2)}) copy-start(f32[32,32,128]{2,0,1:T(8,128)} %get-tuple-element.129) | copy-start | bytes 1572868
  170.9 6.7 %copy-start.50 = (f32[32,32,128]{2,0,1:T(8,128)S(1)}, f32[32,32,128]{2,0,1:T(8,128)}, u32[]{:S(2)}) copy-start(f32[32,32,128]{2,0,1:T(8,128)} %get-tuple-element.131) | copy-start | bytes 1572868
  184.1 46.4 %collective-permute-start.8 = (bf16[32,1,128]{2,0,1:T(8,128)(2,1)}, bf16[32,1,128]{2,0,1:T(8,128)(2,1)}, u32[]{:S(2)}, u32[]{:S(2)}) collective-permute-start(bf16[32,1,128]{2,0,1:T(8,128)(2,1)} %get-tuple-element.116), channel_id=1, source_target_pairs={{0,2},{2,4},{4,6},{6,8},{8,10},{10,12},{12,14},{14,16},{16,18},{18... | collective-permute-start | bytes 24584 | tf_op jit(solution)/shard_map/ppermute | solution.py:13
  228.4 7.3 %collective-permute-start.9 = (bf16[32,1,128]{2,0,1:T(8,128)(2,1)S(1)}, bf16[32,1,128]{2,0,1:T(8,128)(2,1)S(1)}, u32[]{:S(2)}, u32[]{:S(2)}) collective-permute-start(bf16[32,1,128]{2,0,1:T(8,128)(2,1)S(1)} %slice.389), channel_id=1, source_target_pairs={{2,0},{4,2},{6,4},{8,6},{10,8},{12,10},{14,12},{16,14},{18,16},{20... | collective-permute-start | bytes 24584 | tf_op jit(solution)/shard_map/ppermute | solution.py:13
  230.3 5.4 %copy-start.10 = (f32[32,32,128]{2,1,0:T(8,128)S(1)}, f32[32,32,128]{2,1,0:T(8,128)}, u32[]{:S(2)}) copy-start(f32[32,32,128]{2,1,0:T(8,128)} %fusion.143) | copy-start | bytes 1572868
  230.5 5.3 %slice-start.2 = ((bf16[32,32,128]{2,0,1:T(8,128)(2,1)}), bf16[32,31,128]{2,0,1:T(8,128)(2,1)S(1)}, s32[]{:S(2)}) async-start(bf16[32,32,128]{2,0,1:T(8,128)(2,1)} %fusion.28), calls=%async_computation.2 | async-start | bytes 507904 | tf_op jit(solution)/shard_map/slice | solution.py:32
  230.5 6.7 %copy-start.47 = (f32[32,32,128]{2,0,1:T(8,128)S(1)}, f32[32,32,128]{2,0,1:T(8,128)}, u32[]{:S(2)}) copy-start(f32[32,32,128]{2,0,1:T(8,128)} %get-tuple-element.133) | copy-start | bytes 1572868
  242.5 46.4 %collective-permute-start.10 = (bf16[32,1,128]{2,0,1:T(8,128)(2,1)}, bf16[32,1,128]{2,0,1:T(8,128)(2,1)}, u32[]{:S(2)}, u32[]{:S(2)}) collective-permute-start(bf16[32,1,128]{2,0,1:T(8,128)(2,1)} %get-tuple-element.113), channel_id=1, source_target_pairs={{0,2},{2,4},{4,6},{6,8},{8,10},{10,12},{12,14},{14,16},{16,18},{18... | collective-permute-start | bytes 24584 | tf_op jit(solution)/shard_map/ppermute | solution.py:13
  286.6 7.3 %collective-permute-start.11 = (bf16[32,1,128]{2,0,1:T(8,128)(2,1)S(1)}, bf16[32,1,128]{2,0,1:T(8,128)(2,1)S(1)}, u32[]{:S(2)}, u32[]{:S(2)}) collective-permute-start(bf16[32,1,128]{2,0,1:T(8,128)(2,1)S(1)} %slice.395), channel_id=1, source_target_pairs={{2,0},{4,2},{6,4},{8,6},{10,8},{12,10},{14,12},{16,14},{18,16},{20... | collective-permute-start | bytes 24584 | tf_op jit(solution)/shard_map/ppermute | solution.py:13
  288.8 5.2 %copy-start.15 = (f32[32,32,128]{2,1,0:T(8,128)S(1)}, f32[32,32,128]{2,1,0:T(8,128)}, u32[]{:S(2)}) copy-start(f32[32,32,128]{2,1,0:T(8,128)} %fusion.144) | copy-start | bytes 1572868
  288.9 5.1 %slice-start.7 = ((bf16[32,32,128]{2,0,1:T(8,128)(2,1)}), bf16[32,31,128]{2,0,1:T(8,128)(2,1)S(1)}, s32[]{:S(2)}) async-start(bf16[32,32,128]{2,0,1:T(8,128)(2,1)} %fusion.29), calls=%async_computation.7 | async-start | bytes 507904 | tf_op jit(solution)/shard_map/slice | solution.py:32
  288.9 6.5 %copy-start.21 = (f32[32,32,128]{2,0,1:T(8,128)S(1)}, f32[32,32,128]{2,0,1:T(8,128)}, u32[]{:S(2)}) copy-start(f32[32,32,128]{2,0,1:T(8,128)} %copy-done.20) | copy-start | bytes 1572868
  288.9 6.5 %copy-start.48 = (f32[32,32,128]{2,0,1:T(8,128)S(1)}, f32[32,32,128]{2,0,1:T(8,128)}, u32[]{:S(2)}) copy-start(f32[32,32,128]{2,0,1:T(8,128)} %get-tuple-element.133) | copy-start | bytes 1572868
  288.9 6.5 %copy-start.51 = (f32[32,32,128]{2,0,1:T(8,128)S(1)}, f32[32,32,128]{2,0,1:T(8,128)}, u32[]{:S(2)}) copy-start(f32[32,32,128]{2,0,1:T(8,128)} %get-tuple-element.135) | copy-start | bytes 1572868
  301.9 46.3 %collective-permute-start.12 = (bf16[32,1,128]{2,0,1:T(8,128)(2,1)}, bf16[32,1,128]{2,0,1:T(8,128)(2,1)}, u32[]{:S(2)}, u32[]{:S(2)}) collective-permute-start(bf16[32,1,128]{2,0,1:T(8,128)(2,1)} %get-tuple-element.110), channel_id=1, source_target_pairs={{0,2},{2,4},{4,6},{6,8},{8,10},{10,12},{12,14},{14,16},{16,18},{18... | collective-permute-start | bytes 24584 | tf_op jit(solution)/shard_map/ppermute | solution.py:13
  346.1 7.3 %collective-permute-start.13 = (bf16[32,1,128]{2,0,1:T(8,128)(2,1)S(1)}, bf16[32,1,128]{2,0,1:T(8,128)(2,1)S(1)}, u32[]{:S(2)}, u32[]{:S(2)}) collective-permute-start(bf16[32,1,128]{2,0,1:T(8,128)(2,1)S(1)} %slice.401), channel_id=1, source_target_pairs={{2,0},{4,2},{6,4},{8,6},{10,8},{12,10},{14,12},{16,14},{18,16},{20... | collective-permute-start | bytes 24584 | tf_op jit(solution)/shard_map/ppermute | solution.py:13
  348.1 5.4 %copy-start.11 = (f32[32,32,128]{2,1,0:T(8,128)S(1)}, f32[32,32,128]{2,1,0:T(8,128)}, u32[]{:S(2)}) copy-start(f32[32,32,128]{2,1,0:T(8,128)} %fusion.145) | copy-start | bytes 1572868
  348.2 5.3 %slice-start.3 = ((bf16[32,32,128]{2,0,1:T(8,128)(2,1)}), bf16[32,31,128]{2,0,1:T(8,128)(2,1)S(1)}, s32[]{:S(2)}) async-start(bf16[32,32,128]{2,0,1:T(8,128)(2,1)} %fusion.30), calls=%async_computation.3 | async-start | bytes 507904 | tf_op jit(solution)/shard_map/slice | solution.py:32
  348.2 6.7 %copy-start.45 = (f32[32,32,128]{2,0,1:T(8,128)S(1)}, f32[32,32,128]{2,0,1:T(8,128)}, u32[]{:S(2)}) copy-start(f32[32,32,128]{2,0,1:T(8,128)} %get-tuple-element.137) | copy-start | bytes 1572868
  359.6 42.6 %collective-permute-start.14 = (bf16[32,1,128]{2,0,1:T(8,128)(2,1)S(1)}, bf16[32,1,128]{2,0,1:T(8,128)(2,1)S(1)}, u32[]{:S(2)}, u32[]{:S(2)}) collective-permute-start(bf16[32,1,128]{2,0,1:T(8,128)(2,1)S(1)} %get-tuple-element.107), channel_id=1, source_target_pairs={{0,2},{2,4},{4,6},{6,8},{8,10},{10,12},{12,14},{14,16},{16,18},{18... | collective-permute-start | bytes 24584 | tf_op jit(solution)/shard_map/ppermute | solution.py:13
  400.1 7.3 %collective-permute-start.15 = (bf16[32,1,128]{2,0,1:T(8,128)(2,1)S(1)}, bf16[32,1,128]{2,0,1:T(8,128)(2,1)S(1)}, u32[]{:S(2)}, u32[]{:S(2)}) collective-permute-start(bf16[32,1,128]{2,0,1:T(8,128)(2,1)S(1)} %slice.407), channel_id=1, source_target_pairs={{2,0},{4,2},{6,4},{8,6},{10,8},{12,10},{14,12},{16,14},{18,16},{20... | collective-permute-start | bytes 24584 | tf_op jit(solution)/shard_map/ppermute | solution.py:13
  402.1 5.3 %copy-start.12 = (f32[32,32,128]{2,1,0:T(8,128)S(1)}, f32[32,32,128]{2,1,0:T(8,128)}, u32[]{:S(2)}) copy-start(f32[32,32,128]{2,1,0:T(8,128)} %fusion.146) | copy-start | bytes 1572868
  402.2 5.2 %slice-start.4 = ((bf16[32,32,128]{2,0,1:T(8,128)(2,1)}), bf16[32,31,128]{2,0,1:T(8,128)(2,1)S(1)}, s32[]{:S(2)}) async-start(bf16[32,32,128]{2,0,1:T(8,128)(2,1)} %fusion.31), calls=%async_computation.4 | async-start | bytes 507904 | tf_op jit(solution)/shard_map/slice | solution.py:32
  402.2 5.9 %copy-start.23 = (f32[32,32,128]{2,0,1:T(8,128)S(1)}, f32[32,32,128]{2,0,1:T(8,128)}, u32[]{:S(2)}) copy-start(f32[32,32,128]{2,0,1:T(8,128)} %copy-done.22) | copy-start | bytes 1572868
  402.2 5.9 %copy-start.46 = (f32[32,32,128]{2,0,1:T(8,128)S(1)}, f32[32,32,128]{2,0,1:T(8,128)}, u32[]{:S(2)}) copy-start(f32[32,32,128]{2,0,1:T(8,128)} %get-tuple-element.137) | copy-start | bytes 1572868
  402.2 5.9 %copy-start.49 = (f32[32,32,128]{2,0,1:T(8,128)S(1)}, f32[32,32,128]{2,0,1:T(8,128)}, u32[]{:S(2)}) copy-start(f32[32,32,128]{2,0,1:T(8,128)} %get-tuple-element.139) | copy-start | bytes 1572868
  (28 other events, 33.2 us)
where the time goes:
time: 462 us; the launch traced here: 461 us
  blocking collectives  311 us (67%)
  matrix products  43.6 us (9%)
  starting transfers between devices  39.7 us (9%)
  waiting for transfers between devices  36.5 us (8%)
  local copies, waits for them, and re-layouts  22.3 us (5%)
  other arithmetic  5.63 us (1%)
    all_gather x7, blocking collectives, stiffness(): lax.all_gather(field_round[:, :1, :], 'seg', axis=1, tiled=True)  263 us
    psum x1, blocking collectives, body(): grad_total = grad_total + lax.psum(partial_value, ('seg', 'samp'))  48 us
    ppermute x16, starting transfers between devices, shifted(): lax.ppermute(value, axis, [(source, source + steps) for source in range(f...  39.7 us
    ppermute x16, waiting for transfers between devices, shifted(): lax.ppermute(value, axis, [(source, source + steps) for source in range(f...  36.5 us
    dot_general x8, matrix products, stiffness(): jnp.einsum('sjb,jab->sja', field_round, rigidity_diagonal_cells, preferre...  11.7 us
    dot_general x8, matrix products, blockwise(): jnp.einsum('jab,sjb->sja', inverse_diagonal_cells, field_round, preferred...  10.8 us
    gather x8, local copies, waits for them, and re-layouts, stiffness(): jnp.take(interfaces, joined_segment_table[0], axis=1).astype(jnp.float32)  9.89 us
    dot_general x8, matrix products, stiffness(): jnp.einsum('sjb,jab->sja', lower_field, rigidity_lower_cells, preferred_e...  9.37 us
  transfers between devices with their start and end apart: 16, of which 8 were waited for; matrix products, arithmetic and copies ran while one was open for 4% of the time, Pallas kernels for 0%

commit v1 on v0

--- a/solution.py
+++ b/solution.py
@@ -24,7 +24,17 @@
     ).astype(jnp.bfloat16)
     below_rim = shifted(field_round[:, -1:, :], "seg", 1)
     above_rim = shifted(upward[:, :1, :], "seg", -1)
-    interfaces = lax.all_gather(field_round[:, :1, :], "seg", axis=1, tiled=True)
+    shard = field_round[:, :1, :]
+    ways = lax.axis_size("seg")
+    up = [(d, (d + 1) % ways) for d in range(ways)]
+    down = [(d, (d - 1) % ways) for d in range(ways)]
+    earlier, later = ([shard], [shard])
+    for _ in range(ways // 2):
+        earlier.append(lax.ppermute(earlier[-1], "seg", up))
+    for _ in range((ways - 1) // 2):
+        later.append(lax.ppermute(later[-1], "seg", down))
+    line = jnp.concatenate([*earlier[::-1], *later[1:]], axis=1)
+    interfaces = jnp.roll(line, (lax.axis_index("seg") - ways // 2) * shard.shape[1], axis=1)
     lower_field = jnp.concatenate([below_rim, field_round[:, :-1]], axis=1)
     below_term = jnp.einsum(
         "sjb,jab->sja", lower_field, rigidity_lower_cells, preferred_element_type=jnp.float32

time: 462 us -> 596 us (1.29)
  starting transfers between devices: 39.7 us -> 315 us
  blocking collectives: 311 us -> 58.2 us
  waiting for transfers between devices: 36.5 us -> 129 us
  local copies, waits for them, and re-layouts: 22.3 us -> 34.3 us
  other arithmetic: 5.63 us -> 12.4 us
    all_gather x7 -> x0, blocking collectives: 263 us -> none  [stiffness(): lax.all_gather(field_round[:, :1, :], 'seg', axis=1, tiled=True)]
    ppermute x0 -> x120, starting transfers between devices: none -> 259 us  [the longest x56 198 us: stiffness(): later.append(lax.ppermute(later[-1], 'seg', down))]
    ppermute x0 -> x120, waiting for transfers between devices: none -> 103 us  [the longest x64 100 us: stiffness(): earlier.append(lax.ppermute(earlier[-1], 'seg', up))]
    ppermute x16, starting transfers between devices: 39.7 us -> 55.9 us  [shifted(): lax.ppermute(value, axis, [(source, source + steps) for source in range(f...]
    ppermute x16, waiting for transfers between devices: 36.5 us -> 25.6 us  [shifted(): lax.ppermute(value, axis, [(source, source + steps) for source in range(f...]
    psum x1, blocking collectives: 48 us -> 58.2 us  [body(): grad_total = grad_total + lax.psum(partial_value, ('seg', 'samp'))]
  transfers between devices with their start and end apart: 16 -> 136, of which waited for: 8 -> 68; matrix products, arithmetic and copies ran while one was open for 4% -> 9% of each run, Pallas kernels for 0% -> 0%
where the time goes in v1:
time: 596 us; the launch traced here: 594 us
  starting transfers between devices  315 us (53%)
  waiting for transfers between devices  129 us (22%)
  blocking collectives  58.2 us (10%)
  matrix products  43.2 us (7%)
  local copies, waits for them, and re-layouts  34.3 us (6%)
  other arithmetic  12.4 us (2%)
    ppermute x56, starting transfers between devices, stiffness(): later.append(lax.ppermute(later[-1], 'seg', down))  198 us
    ppermute x64, waiting for transfers between devices, stiffness(): earlier.append(lax.ppermute(earlier[-1], 'seg', up))  100 us
    ppermute x64, starting transfers between devices, stiffness(): earlier.append(lax.ppermute(earlier[-1], 'seg', up))  61 us
    psum x1, blocking collectives, body(): grad_total = grad_total + lax.psum(partial_value, ('seg', 'samp'))  58.2 us
    ppermute x16, starting transfers between devices, shifted(): lax.ppermute(value, axis, [(source, source + steps) for source in range(f...  55.9 us
    ppermute x16, waiting for transfers between devices, shifted(): lax.ppermute(value, axis, [(source, source + steps) for source in range(f...  25.6 us
    dot_general x8, matrix products, stiffness(): jnp.einsum('sjb,jab->sja', lower_field, rigidity_lower_cells, preferred_e...  14.1 us
  transfers between devices with their start and end apart: 136, of which 68 were waited for; matrix products, arithmetic and copies ran while one was open for 9% of the time, Pallas kernels for 0%

profile of v1, /device:TPU:14, one launch (start us, length us, event | category | flops | bytes accessed | tf_op | source)
XLA Modules:
  0.0 593.7 jit_solution(3332813545086737417)
XLA Ops:
  8.0 4.0 collective-permute-start.1
  20.7 4.1 collective-permute-start.5
  26.2 4.1 collective-permute-start.6
  31.7 4.1 collective-permute-start.7
  37.1 4.2 collective-permute-start.8
  42.9 4.2 collective-permute-start.9
  63.7 4.1 collective-permute-start.20
  69.2 4.1 collective-permute-start.21
  74.6 4.1 collective-permute-start.22
  80.1 4.1 collective-permute-start.23
  85.5 4.1 collective-permute-start.24
  91.0 4.1 collective-permute-start.25
  96.5 4.0 collective-permute-start.26
  104.1 4.7 collective-permute-start.33
  114.0 5.0 collective-permute-done.17
  122.4 7.2 %collective-permute-done.36 = bf16[32,1,128]{2,0,1:T(8,128)(2,1)S(1)} collective-permute-done((bf16[32,1,128]{2,0,1:T(8,128)(2,1)S(1)}, bf16[32,1,128]{2,0,1:T(8,128)(2,1)S(1)}, u32[]{:S(2)}, u32[]{:S(2)}) %collective-permute-start.36) | collective-permute-done | bytes 8224 | tf_op jit(solution)/shard_map/ppermute | solution.py:33
  129.7 5.6 collective-permute-start.44
  136.9 5.7 collective-permute-start.45
  144.2 5.6 collective-permute-start.46
  170.2 5.7 collective-permute-start.35
  192.1 6.9 %collective-permute-done.53 = bf16[32,1,128]{2,0,1:T(8,128)(2,1)S(1)} collective-permute-done((bf16[32,1,128]{2,0,1:T(8,128)(2,1)S(1)}, bf16[32,1,128]{2,0,1:T(8,128)(2,1)S(1)}, u32[]{:S(2)}, u32[]{:S(2)}) %collective-permute-start.53) | collective-permute-done | bytes 8224 | tf_op jit(solution)/shard_map/ppermute | solution.py:33
  199.0 5.6 collective-permute-start.61
  206.2 5.6 collective-permute-start.62
  213.4 5.6 collective-permute-start.63
  239.5 5.7 collective-permute-start.52
  261.4 6.2 %collective-permute-done.70 = bf16[32,1,128]{2,0,1:T(8,128)(2,1)S(1)} collective-permute-done((bf16[32,1,128]{2,0,1:T(8,128)(2,1)S(1)}, bf16[32,1,128]{2,0,1:T(8,128)(2,1)S(1)}, u32[]{:S(2)}, u32[]{:S(2)}) %collective-permute-start.70) | collective-permute-done | bytes 8224 | tf_op jit(solution)/shard_map/ppermute | solution.py:33
  267.6 5.7 collective-permute-start.78
  274.9 5.5 collective-permute-start.79
  282.1 5.6 collective-permute-start.80
  308.1 5.7 collective-permute-start.69
  330.0 6.3 %collective-permute-done.87 = bf16[32,1,128]{2,0,1:T(8,128)(2,1)S(1)} collective-permute-done((bf16[32,1,128]{2,0,1:T(8,128)(2,1)S(1)}, bf16[32,1,128]{2,0,1:T(8,128)(2,1)S(1)}, u32[]{:S(2)}, u32[]{:S(2)}) %collective-permute-start.87) | collective-permute-done | bytes 8224 | tf_op jit(solution)/shard_map/ppermute | solution.py:33
  336.3 5.6 collective-permute-start.95
  343.6 5.6 collective-permute-start.96
  350.8 5.6 collective-permute-start.97
  376.8 5.7 collective-permute-start.86
  382.6 3.9 collective-permute-start.101
  398.8 6.2 %collective-permute-done.104 = bf16[32,1,128]{2,0,1:T(8,128)(2,1)S(1)} collective-permute-done((bf16[32,1,128]{2,0,1:T(8,128)(2,1)S(1)}, bf16[32,1,128]{2,0,1:T(8,128)(2,1)S(1)}, u32[]{:S(2)}, u32[]{:S(2)}) %collective-permute-start.104) | collective-permute-done | bytes 8224 | tf_op jit(solution)/shard_map/ppermute | solution.py:33
  405.0 5.6 collective-permute-start.112
  412.2 5.6 collective-permute-start.113
  419.5 5.6 collective-permute-start.114
  445.5 5.7 collective-permute-start.103
  467.9 5.8 collective-permute-done.121
  473.8 5.6 collective-permute-start.129
  481.5 5.7 collective-permute-start.130
  488.5 5.6 collective-permute-start.131
  512.9 5.8 collective-permute-start.120
  526.2 4.7 collective-permute-done.119
  534.9 58.2 %psum.34 = f32[512]{0:T(512)S(1)} all-reduce(f32[512]{0:T(512)S(1)} %add_add_fusion), channel_id=1, replica_groups=mesh['seg'=16,'samp'=2] {'seg','samp'}, use_global_device_ids=true, to_apply=%region_9.12 | all-reduce | flops 512 | bytes 4096 | tf_op jit(solution)/shard_map/psum | solution.py:136
  (562 shorter events, 287.9 us)
Async XLA Ops:
  1.3 18.2 %collective-permute-start.10 = (bf16[32,1,128]{2,0,1:T(8,128)(2,1)}, bf16[32,1,128]{2,0,1:T(8,128)(2,1)S(1)}, u32[]{:S(2)}, u32[]{:S(2)}) collective-permute-start(bf16[32,1,128]{2,0,1:T(8,128)(2,1)} %slice.300), channel_id=1, source_target_pairs={{0,30},{2,0},{4,2},{6,4},{8,6},{10,8},{12,10},{14,12},{16,14},{18,... | collective-permute-start | bytes 24584 | tf_op jit(solution)/shard_map/ppermute | solution.py:35
  1.8 10.3 %collective-permute-start.2 = (bf16[32,1,128]{2,0,1:T(8,128)(2,1)}, bf16[32,1,128]{2,0,1:T(8,128)(2,1)S(1)}, u32[]{:S(2)}, u32[]{:S(2)}) collective-permute-start(bf16[32,1,128]{2,0,1:T(8,128)(2,1)} %slice.300), channel_id=1, source_target_pairs={{0,2},{2,4},{4,6},{6,8},{8,10},{10,12},{12,14},{14,16},{16,18},{18... | collective-permute-start | bytes 24584 | tf_op jit(solution)/shard_map/ppermute | solution.py:33
  5.1 42.0 %collective-permute-start = (bf16[32,1,128]{2,0,1:T(8,128)(2,1)}, bf16[32,1,128]{2,0,1:T(8,128)(2,1)S(1)}, u32[]{:S(2)}, u32[]{:S(2)}) collective-permute-start(bf16[32,1,128]{2,0,1:T(8,128)(2,1)} %slice.300), channel_id=1, source_target_pairs={{0,2},{2,4},{4,6},{6,8},{8,10},{10,12},{12,14},{14,16},{16,18},{18... | collective-permute-start | bytes 24584 | tf_op jit(solution)/shard_map/ppermute | solution.py:13
  8.0 39.1 %collective-permute-start.1 = (bf16[32,1,128]{2,0,1:T(8,128)(2,1)}, bf16[32,1,128]{2,0,1:T(8,128)(2,1)S(1)}, u32[]{:S(2)}, u32[]{:S(2)}) collective-permute-start(bf16[32,1,128]{2,0,1:T(8,128)(2,1)} %slice.363), channel_id=1, source_target_pairs={{2,0},{4,2},{6,4},{8,6},{10,8},{12,10},{14,12},{16,14},{18,16},{20... | collective-permute-start | bytes 24584 | tf_op jit(solution)/shard_map/ppermute | solution.py:13
  41.8 7.8 %collective-permute-start.15 = (bf16[32,1,128]{2,0,1:T(8,128)(2,1)}, bf16[32,1,128]{2,0,1:T(8,128)(2,1)S(1)}, u32[]{:S(2)}, u32[]{:S(2)}) collective-permute-start(bf16[32,1,128]{2,0,1:T(8,128)(2,1)} %collective-permute-done.14), channel_id=1, source_target_pairs={{0,30},{2,0},{4,2},{6,4},{8,6},{10,8},{12,10},{14,12},{16,14},{18,... | collective-permute-start | bytes 24584 | tf_op jit(solution)/shard_map/ppermute | solution.py:35
  96.5 7.6 %collective-permute-start.32 = (bf16[32,1,128]{2,0,1:T(8,128)(2,1)S(1)}, bf16[32,1,128]{2,0,1:T(8,128)(2,1)S(1)}, u32[]{:S(2)}, u32[]{:S(2)}) collective-permute-start(bf16[32,1,128]{2,0,1:T(8,128)(2,1)S(1)} %collective-permute-done.31), channel_id=1, source_target_pairs={{0,30},{2,0},{4,2},{6,4},{8,6},{10,8},{12,10},{14,12},{16,14},{18,... | collective-permute-start | bytes 24584 | tf_op jit(solution)/shard_map/ppermute | solution.py:35
  96.5 12.3 %collective-permute-start.26 = (bf16[32,1,128]{2,0,1:T(8,128)(2,1)S(1)}, bf16[32,1,128]{2,0,1:T(8,128)(2,1)S(1)}, u32[]{:S(2)}, u32[]{:S(2)}) collective-permute-start(bf16[32,1,128]{2,0,1:T(8,128)(2,1)S(1)} %collective-permute-done.25), channel_id=1, source_target_pairs={{0,2},{2,4},{4,6},{6,8},{8,10},{10,12},{12,14},{14,16},{16,18},{18... | collective-permute-start | bytes 24584 | tf_op jit(solution)/shard_map/ppermute | solution.py:33
  102.2 11.8 %collective-permute-start.18 = (bf16[32,1,128]{2,0,1:T(8,128)(2,1)}, bf16[32,1,128]{2,0,1:T(8,128)(2,1)}, u32[]{:S(2)}, u32[]{:S(2)}) collective-permute-start(bf16[32,1,128]{2,0,1:T(8,128)(2,1)} %slice.368), channel_id=1, source_target_pairs={{2,0},{4,2},{6,4},{8,6},{10,8},{12,10},{14,12},{16,14},{18,16},{20... | collective-permute-start | bytes 24584 | tf_op jit(solution)/shard_map/ppermute | solution.py:13
  104.1 7.5 %collective-permute-start.33 = (bf16[32,1,128]{2,0,1:T(8,128)(2,1)S(1)}, bf16[32,1,128]{2,0,1:T(8,128)(2,1)S(1)}, u32[]{:S(2)}, u32[]{:S(2)}) collective-permute-start(bf16[32,1,128]{2,0,1:T(8,128)(2,1)S(1)} %collective-permute-done.32), channel_id=1, source_target_pairs={{0,30},{2,0},{4,2},{6,4},{8,6},{10,8},{12,10},{14,12},{16,14},{18,... | collective-permute-start | bytes 24584 | tf_op jit(solution)/shard_map/ppermute | solution.py:35
  109.5 9.5 %collective-permute-start.17 = (bf16[32,1,128]{2,0,1:T(8,128)(2,1)}, bf16[32,1,128]{2,0,1:T(8,128)(2,1)S(1)}, u32[]{:S(2)}, u32[]{:S(2)}) collective-permute-start(bf16[32,1,128]{2,0,1:T(8,128)(2,1)} %get-tuple-element.124), channel_id=1, source_target_pairs={{0,2},{2,4},{4,6},{6,8},{8,10},{10,12},{12,14},{14,16},{16,18},{18... | collective-permute-start | bytes 24584 | tf_op jit(solution)/shard_map/ppermute | solution.py:13
  129.7 7.2 %collective-permute-start.44 = (bf16[32,1,128]{2,0,1:T(8,128)(2,1)S(1)}, bf16[32,1,128]{2,0,1:T(8,128)(2,1)S(1)}, u32[]{:S(2)}, u32[]{:S(2)}) collective-permute-start(bf16[32,1,128]{2,0,1:T(8,128)(2,1)S(1)} %slice.376), channel_id=1, source_target_pairs={{0,30},{2,0},{4,2},{6,4},{8,6},{10,8},{12,10},{14,12},{16,14},{18,... | collective-permute-start | bytes 24584 | tf_op jit(solution)/shard_map/ppermute | solution.py:35
  136.9 7.3 %collective-permute-start.38 = (bf16[32,1,128]{2,0,1:T(8,128)(2,1)S(1)}, bf16[32,1,128]{2,0,1:T(8,128)(2,1)S(1)}, u32[]{:S(2)}, u32[]{:S(2)}) collective-permute-start(bf16[32,1,128]{2,0,1:T(8,128)(2,1)S(1)} %collective-permute-done.37), channel_id=1, source_target_pairs={{0,2},{2,4},{4,6},{6,8},{8,10},{10,12},{12,14},{14,16},{16,18},{18... | collective-permute-start | bytes 24584 | tf_op jit(solution)/shard_map/ppermute | solution.py:33
  136.9 7.3 %collective-permute-start.45 = (bf16[32,1,128]{2,0,1:T(8,128)(2,1)S(1)}, bf16[32,1,128]{2,0,1:T(8,128)(2,1)S(1)}, u32[]{:S(2)}, u32[]{:S(2)}) collective-permute-start(bf16[32,1,128]{2,0,1:T(8,128)(2,1)S(1)} %collective-permute-done.44), channel_id=1, source_target_pairs={{0,30},{2,0},{4,2},{6,4},{8,6},{10,8},{12,10},{14,12},{16,14},{18,... | collective-permute-start | bytes 24584 | tf_op jit(solution)/shard_map/ppermute | solution.py:35
  163.8 12.1 %collective-permute-start.49 = (bf16[32,1,128]{2,0,1:T(8,128)(2,1)S(1)}, bf16[32,1,128]{2,0,1:T(8,128)(2,1)S(1)}, u32[]{:S(2)}, u32[]{:S(2)}) collective-permute-start(bf16[32,1,128]{2,0,1:T(8,128)(2,1)S(1)} %collective-permute-done.48), channel_id=1, source_target_pairs={{0,30},{2,0},{4,2},{6,4},{8,6},{10,8},{12,10},{14,12},{16,14},{18,... | collective-permute-start | bytes 24584 | tf_op jit(solution)/shard_map/ppermute | solution.py:35
  167.7 12.0 %collective-permute-start.43 = (bf16[32,1,128]{2,0,1:T(8,128)(2,1)S(1)}, bf16[32,1,128]{2,0,1:T(8,128)(2,1)S(1)}, u32[]{:S(2)}, u32[]{:S(2)}) collective-permute-start(bf16[32,1,128]{2,0,1:T(8,128)(2,1)S(1)} %collective-permute-done.42), channel_id=1, source_target_pairs={{0,2},{2,4},{4,6},{6,8},{8,10},{10,12},{12,14},{14,16},{16,18},{18... | collective-permute-start | bytes 24584 | tf_op jit(solution)/shard_map/ppermute | solution.py:33
  170.2 14.6 %collective-permute-start.35 = (bf16[32,1,128]{2,0,1:T(8,128)(2,1)}, bf16[32,1,128]{2,0,1:T(8,128)(2,1)S(1)}, u32[]{:S(2)}, u32[]{:S(2)}) collective-permute-start(bf16[32,1,128]{2,0,1:T(8,128)(2,1)} %slice.374), channel_id=1, source_target_pairs={{2,0},{4,2},{6,4},{8,6},{10,8},{12,10},{14,12},{16,14},{18,16},{20... | collective-permute-start | bytes 24584 | tf_op jit(solution)/shard_map/ppermute | solution.py:13
  180.5 7.5 %collective-permute-start.34 = (bf16[32,1,128]{2,0,1:T(8,128)(2,1)}, bf16[32,1,128]{2,0,1:T(8,128)(2,1)S(1)}, u32[]{:S(2)}, u32[]{:S(2)}) collective-permute-start(bf16[32,1,128]{2,0,1:T(8,128)(2,1)} %get-tuple-element.121), channel_id=1, source_target_pairs={{0,2},{2,4},{4,6},{6,8},{8,10},{10,12},{12,14},{14,16},{16,18},{18... | collective-permute-start | bytes 24584 | tf_op jit(solution)/shard_map/ppermute | solution.py:13
  213.4 7.3 %collective-permute-start.56 = (bf16[32,1,128]{2,0,1:T(8,128)(2,1)S(1)}, bf16[32,1,128]{2,0,1:T(8,128)(2,1)S(1)}, u32[]{:S(2)}, u32[]{:S(2)}) collective-permute-start(bf16[32,1,128]{2,0,1:T(8,128)(2,1)S(1)} %collective-permute-done.55), channel_id=1, source_target_pairs={{0,2},{2,4},{4,6},{6,8},{8,10},{10,12},{12,14},{14,16},{16,18},{18... | collective-permute-start | bytes 24584 | tf_op jit(solution)/shard_map/ppermute | solution.py:33
  213.4 7.3 %collective-permute-start.63 = (bf16[32,1,128]{2,0,1:T(8,128)(2,1)S(1)}, bf16[32,1,128]{2,0,1:T(8,128)(2,1)S(1)}, u32[]{:S(2)}, u32[]{:S(2)}) collective-permute-start(bf16[32,1,128]{2,0,1:T(8,128)(2,1)S(1)} %collective-permute-done.62), channel_id=1, source_target_pairs={{0,30},{2,0},{4,2},{6,4},{8,6},{10,8},{12,10},{14,12},{16,14},{18,... | collective-permute-start | bytes 24584 | tf_op jit(solution)/shard_map/ppermute | solution.py:35
  233.1 12.1 %collective-permute-start.66 = (bf16[32,1,128]{2,0,1:T(8,128)(2,1)S(1)}, bf16[32,1,128]{2,0,1:T(8,128)(2,1)S(1)}, u32[]{:S(2)}, u32[]{:S(2)}) collective-permute-start(bf16[32,1,128]{2,0,1:T(8,128)(2,1)S(1)} %collective-permute-done.65), channel_id=1, source_target_pairs={{0,30},{2,0},{4,2},{6,4},{8,6},{10,8},{12,10},{14,12},{16,14},{18,... | collective-permute-start | bytes 24584 | tf_op jit(solution)/shard_map/ppermute | solution.py:35
  237.0 12.0 %collective-permute-start.60 = (bf16[32,1,128]{2,0,1:T(8,128)(2,1)S(1)}, bf16[32,1,128]{2,0,1:T(8,128)(2,1)S(1)}, u32[]{:S(2)}, u32[]{:S(2)}) collective-permute-start(bf16[32,1,128]{2,0,1:T(8,128)(2,1)S(1)} %collective-permute-done.59), channel_id=1, source_target_pairs={{0,2},{2,4},{4,6},{6,8},{8,10},{10,12},{12,14},{14,16},{16,18},{18... | collective-permute-start | bytes 24584 | tf_op jit(solution)/shard_map/ppermute | solution.py:33
  239.5 14.6 %collective-permute-start.52 = (bf16[32,1,128]{2,0,1:T(8,128)(2,1)}, bf16[32,1,128]{2,0,1:T(8,128)(2,1)S(1)}, u32[]{:S(2)}, u32[]{:S(2)}) collective-permute-start(bf16[32,1,128]{2,0,1:T(8,128)(2,1)} %slice.380), channel_id=1, source_target_pairs={{2,0},{4,2},{6,4},{8,6},{10,8},{12,10},{14,12},{16,14},{18,16},{20... | collective-permute-start | bytes 24584 | tf_op jit(solution)/shard_map/ppermute | solution.py:13
  249.7 7.6 %collective-permute-start.51 = (bf16[32,1,128]{2,0,1:T(8,128)(2,1)}, bf16[32,1,128]{2,0,1:T(8,128)(2,1)S(1)}, u32[]{:S(2)}, u32[]{:S(2)}) collective-permute-start(bf16[32,1,128]{2,0,1:T(8,128)(2,1)} %get-tuple-element.118), channel_id=1, source_target_pairs={{0,2},{2,4},{4,6},{6,8},{8,10},{10,12},{12,14},{14,16},{16,18},{18... | collective-permute-start | bytes 24584 | tf_op jit(solution)/shard_map/ppermute | solution.py:13
  267.6 7.3 %collective-permute-start.71 = (bf16[32,1,128]{2,0,1:T(8,128)(2,1)S(1)}, bf16[32,1,128]{2,0,1:T(8,128)(2,1)S(1)}, u32[]{:S(2)}, u32[]{:S(2)}) collective-permute-start(bf16[32,1,128]{2,0,1:T(8,128)(2,1)S(1)} %collective-permute-done.70), channel_id=1, source_target_pairs={{0,2},{2,4},{4,6},{6,8},{8,10},{10,12},{12,14},{14,16},{16,18},{18... | collective-permute-start | bytes 24584 | tf_op jit(solution)/shard_map/ppermute | solution.py:33
  267.6 7.3 %collective-permute-start.78 = (bf16[32,1,128]{2,0,1:T(8,128)(2,1)S(1)}, bf16[32,1,128]{2,0,1:T(8,128)(2,1)S(1)}, u32[]{:S(2)}, u32[]{:S(2)}) collective-permute-start(bf16[32,1,128]{2,0,1:T(8,128)(2,1)S(1)} %slice.388), channel_id=1, source_target_pairs={{0,30},{2,0},{4,2},{6,4},{8,6},{10,8},{12,10},{14,12},{16,14},{18,... | collective-permute-start | bytes 24584 | tf_op jit(solution)/shard_map/ppermute | solution.py:35
  301.7 12.1 %collective-permute-start.83 = (bf16[32,1,128]{2,0,1:T(8,128)(2,1)S(1)}, bf16[32,1,128]{2,0,1:T(8,128)(2,1)S(1)}, u32[]{:S(2)}, u32[]{:S(2)}) collective-permute-start(bf16[32,1,128]{2,0,1:T(8,128)(2,1)S(1)} %collective-permute-done.82), channel_id=1, source_target_pairs={{0,30},{2,0},{4,2},{6,4},{8,6},{10,8},{12,10},{14,12},{16,14},{18,... | collective-permute-start | bytes 24584 | tf_op jit(solution)/shard_map/ppermute | solution.py:35
  305.6 12.0 %collective-permute-start.77 = (bf16[32,1,128]{2,0,1:T(8,128)(2,1)S(1)}, bf16[32,1,128]{2,0,1:T(8,128)(2,1)S(1)}, u32[]{:S(2)}, u32[]{:S(2)}) collective-permute-start(bf16[32,1,128]{2,0,1:T(8,128)(2,1)S(1)} %collective-permute-done.76), channel_id=1, source_target_pairs={{0,2},{2,4},{4,6},{6,8},{8,10},{10,12},{12,14},{14,16},{16,18},{18... | collective-permute-start | bytes 24584 | tf_op jit(solution)/shard_map/ppermute | solution.py:33
  308.1 14.6 %collective-permute-start.69 = (bf16[32,1,128]{2,0,1:T(8,128)(2,1)}, bf16[32,1,128]{2,0,1:T(8,128)(2,1)S(1)}, u32[]{:S(2)}, u32[]{:S(2)}) collective-permute-start(bf16[32,1,128]{2,0,1:T(8,128)(2,1)} %slice.386), channel_id=1, source_target_pairs={{2,0},{4,2},{6,4},{8,6},{10,8},{12,10},{14,12},{16,14},{18,16},{20... | collective-permute-start | bytes 24584 | tf_op jit(solution)/shard_map/ppermute | solution.py:13
  318.4 7.5 %collective-permute-start.68 = (bf16[32,1,128]{2,0,1:T(8,128)(2,1)}, bf16[32,1,128]{2,0,1:T(8,128)(2,1)S(1)}, u32[]{:S(2)}, u32[]{:S(2)}) collective-permute-start(bf16[32,1,128]{2,0,1:T(8,128)(2,1)} %get-tuple-element.115), channel_id=1, source_target_pairs={{0,2},{2,4},{4,6},{6,8},{8,10},{10,12},{12,14},{14,16},{16,18},{18... | collective-permute-start | bytes 24584 | tf_op jit(solution)/shard_map/ppermute | solution.py:13
  336.3 7.2 %collective-permute-start.95 = (bf16[32,1,128]{2,0,1:T(8,128)(2,1)S(1)}, bf16[32,1,128]{2,0,1:T(8,128)(2,1)S(1)}, u32[]{:S(2)}, u32[]{:S(2)}) collective-permute-start(bf16[32,1,128]{2,0,1:T(8,128)(2,1)S(1)} %slice.394), channel_id=1, source_target_pairs={{0,30},{2,0},{4,2},{6,4},{8,6},{10,8},{12,10},{14,12},{16,14},{18,... | collective-permute-start | bytes 24584 | tf_op jit(solution)/shard_map/ppermute | solution.py:35
  370.4 12.1 %collective-permute-start.100 = (bf16[32,1,128]{2,0,1:T(8,128)(2,1)S(1)}, bf16[32,1,128]{2,0,1:T(8,128)(2,1)S(1)}, u32[]{:S(2)}, u32[]{:S(2)}) collective-permute-start(bf16[32,1,128]{2,0,1:T(8,128)(2,1)S(1)} %collective-permute-done.99), channel_id=1, source_target_pairs={{0,30},{2,0},{4,2},{6,4},{8,6},{10,8},{12,10},{14,12},{16,14},{18,... | collective-permute-start | bytes 24584 | tf_op jit(solution)/shard_map/ppermute | solution.py:35
  374.4 12.0 %collective-permute-start.94 = (bf16[32,1,128]{2,0,1:T(8,128)(2,1)S(1)}, bf16[32,1,128]{2,0,1:T(8,128)(2,1)S(1)}, u32[]{:S(2)}, u32[]{:S(2)}) collective-permute-start(bf16[32,1,128]{2,0,1:T(8,128)(2,1)S(1)} %collective-permute-done.93), channel_id=1, source_target_pairs={{0,2},{2,4},{4,6},{6,8},{8,10},{10,12},{12,14},{14,16},{16,18},{18... | collective-permute-start | bytes 24584 | tf_op jit(solution)/shard_map/ppermute | solution.py:33
  376.8 14.6 %collective-permute-start.86 = (bf16[32,1,128]{2,0,1:T(8,128)(2,1)}, bf16[32,1,128]{2,0,1:T(8,128)(2,1)S(1)}, u32[]{:S(2)}, u32[]{:S(2)}) collective-permute-start(bf16[32,1,128]{2,0,1:T(8,128)(2,1)} %slice.392), channel_id=1, source_target_pairs={{2,0},{4,2},{6,4},{8,6},{10,8},{12,10},{14,12},{16,14},{18,16},{20... | collective-permute-start | bytes 24584 | tf_op jit(solution)/shard_map/ppermute | solution.py:13
  387.1 7.5 %collective-permute-start.85 = (bf16[32,1,128]{2,0,1:T(8,128)(2,1)}, bf16[32,1,128]{2,0,1:T(8,128)(2,1)S(1)}, u32[]{:S(2)}, u32[]{:S(2)}) collective-permute-start(bf16[32,1,128]{2,0,1:T(8,128)(2,1)} %get-tuple-element.112), channel_id=1, source_target_pairs={{0,2},{2,4},{4,6},{6,8},{8,10},{10,12},{12,14},{14,16},{16,18},{18... | collective-permute-start | bytes 24584 | tf_op jit(solution)/shard_map/ppermute | solution.py:13
  405.0 7.3 %collective-permute-start.105 = (bf16[32,1,128]{2,0,1:T(8,128)(2,1)S(1)}, bf16[32,1,128]{2,0,1:T(8,128)(2,1)S(1)}, u32[]{:S(2)}, u32[]{:S(2)}) collective-permute-start(bf16[32,1,128]{2,0,1:T(8,128)(2,1)S(1)} %collective-permute-done.104), channel_id=1, source_target_pairs={{0,2},{2,4},{4,6},{6,8},{8,10},{10,12},{12,14},{14,16},{16,18},{18... | collective-permute-start | bytes 24584 | tf_op jit(solution)/shard_map/ppermute | solution.py:33
  405.0 7.3 %collective-permute-start.112 = (bf16[32,1,128]{2,0,1:T(8,128)(2,1)S(1)}, bf16[32,1,128]{2,0,1:T(8,128)(2,1)S(1)}, u32[]{:S(2)}, u32[]{:S(2)}) collective-permute-start(bf16[32,1,128]{2,0,1:T(8,128)(2,1)S(1)} %slice.400), channel_id=1, source_target_pairs={{0,30},{2,0},{4,2},{6,4},{8,6},{10,8},{12,10},{14,12},{16,14},{18,... | collective-permute-start | bytes 24584 | tf_op jit(solution)/shard_map/ppermute | solution.py:35
  412.2 7.3 %collective-permute-start.106 = (bf16[32,1,128]{2,0,1:T(8,128)(2,1)S(1)}, bf16[32,1,128]{2,0,1:T(8,128)(2,1)S(1)}, u32[]{:S(2)}, u32[]{:S(2)}) collective-permute-start(bf16[32,1,128]{2,0,1:T(8,128)(2,1)S(1)} %collective-permute-done.105), channel_id=1, source_target_pairs={{0,2},{2,4},{4,6},{6,8},{8,10},{10,12},{12,14},{14,16},{16,18},{18... | collective-permute-start | bytes 24584 | tf_op jit(solution)/shard_map/ppermute | solution.py:33
  412.2 7.3 %collective-permute-start.113 = (bf16[32,1,128]{2,0,1:T(8,128)(2,1)S(1)}, bf16[32,1,128]{2,0,1:T(8,128)(2,1)S(1)}, u32[]{:S(2)}, u32[]{:S(2)}) collective-permute-start(bf16[32,1,128]{2,0,1:T(8,128)(2,1)S(1)} %collective-permute-done.112), channel_id=1, source_target_pairs={{0,30},{2,0},{4,2},{6,4},{8,6},{10,8},{12,10},{14,12},{16,14},{18,... | collective-permute-start | bytes 24584 | tf_op jit(solution)/shard_map/ppermute | solution.py:35
  439.1 12.1 %collective-permute-start.117 = (bf16[32,1,128]{2,0,1:T(8,128)(2,1)S(1)}, bf16[32,1,128]{2,0,1:T(8,128)(2,1)S(1)}, u32[]{:S(2)}, u32[]{:S(2)}) collective-permute-start(bf16[32,1,128]{2,0,1:T(8,128)(2,1)S(1)} %collective-permute-done.116), channel_id=1, source_target_pairs={{0,30},{2,0},{4,2},{6,4},{8,6},{10,8},{12,10},{14,12},{16,14},{18,... | collective-permute-start | bytes 24584 | tf_op jit(solution)/shard_map/ppermute | solution.py:35
  443.1 12.0 %collective-permute-start.111 = (bf16[32,1,128]{2,0,1:T(8,128)(2,1)S(1)}, bf16[32,1,128]{2,0,1:T(8,128)(2,1)S(1)}, u32[]{:S(2)}, u32[]{:S(2)}) collective-permute-start(bf16[32,1,128]{2,0,1:T(8,128)(2,1)S(1)} %collective-permute-done.110), channel_id=1, source_target_pairs={{0,2},{2,4},{4,6},{6,8},{8,10},{10,12},{12,14},{14,16},{16,18},{18... | collective-permute-start | bytes 24584 | tf_op jit(solution)/shard_map/ppermute | solution.py:33
  445.5 14.9 %collective-permute-start.103 = (bf16[32,1,128]{2,0,1:T(8,128)(2,1)}, bf16[32,1,128]{2,0,1:T(8,128)(2,1)S(1)}, u32[]{:S(2)}, u32[]{:S(2)}) collective-permute-start(bf16[32,1,128]{2,0,1:T(8,128)(2,1)} %slice.398), channel_id=1, source_target_pairs={{2,0},{4,2},{6,4},{8,6},{10,8},{12,10},{14,12},{16,14},{18,16},{20... | collective-permute-start | bytes 24584 | tf_op jit(solution)/shard_map/ppermute | solution.py:13
  455.8 7.5 %collective-permute-start.102 = (bf16[32,1,128]{2,0,1:T(8,128)(2,1)}, bf16[32,1,128]{2,0,1:T(8,128)(2,1)S(1)}, u32[]{:S(2)}, u32[]{:S(2)}) collective-permute-start(bf16[32,1,128]{2,0,1:T(8,128)(2,1)} %get-tuple-element.109), channel_id=1, source_target_pairs={{0,2},{2,4},{4,6},{6,8},{8,10},{10,12},{12,14},{14,16},{16,18},{18... | collective-permute-start | bytes 24584 | tf_op jit(solution)/shard_map/ppermute | solution.py:13
  473.8 7.6 %collective-permute-start.129 = (bf16[32,1,128]{2,0,1:T(8,128)(2,1)S(1)}, bf16[32,1,128]{2,0,1:T(8,128)(2,1)S(1)}, u32[]{:S(2)}, u32[]{:S(2)}) collective-permute-start(bf16[32,1,128]{2,0,1:T(8,128)(2,1)S(1)} %slice.406), channel_id=1, source_target_pairs={{0,30},{2,0},{4,2},{6,4},{8,6},{10,8},{12,10},{14,12},{16,14},{18,... | collective-permute-start | bytes 24584 | tf_op jit(solution)/shard_map/ppermute | solution.py:35
  488.5 7.5 %collective-permute-start.131 = (bf16[32,1,128]{2,0,1:T(8,128)(2,1)S(1)}, bf16[32,1,128]{2,0,1:T(8,128)(2,1)S(1)}, u32[]{:S(2)}, u32[]{:S(2)}) collective-permute-start(bf16[32,1,128]{2,0,1:T(8,128)(2,1)S(1)} %collective-permute-done.130), channel_id=1, source_target_pairs={{0,30},{2,0},{4,2},{6,4},{8,6},{10,8},{12,10},{14,12},{16,14},{18,... | collective-permute-start | bytes 24584 | tf_op jit(solution)/shard_map/ppermute | solution.py:35
  507.8 11.0 %collective-permute-start.134 = (bf16[32,1,128]{2,0,1:T(8,128)(2,1)S(1)}, bf16[32,1,128]{2,0,1:T(8,128)(2,1)S(1)}, u32[]{:S(2)}, u32[]{:S(2)}) collective-permute-start(bf16[32,1,128]{2,0,1:T(8,128)(2,1)S(1)} %collective-permute-done.133), channel_id=1, source_target_pairs={{0,30},{2,0},{4,2},{6,4},{8,6},{10,8},{12,10},{14,12},{16,14},{18,... | collective-permute-start | bytes 24584 | tf_op jit(solution)/shard_map/ppermute | solution.py:35
  511.8 10.9 %collective-permute-start.128 = (bf16[32,1,128]{2,0,1:T(8,128)(2,1)S(1)}, bf16[32,1,128]{2,0,1:T(8,128)(2,1)S(1)}, u32[]{:S(2)}, u32[]{:S(2)}) collective-permute-start(bf16[32,1,128]{2,0,1:T(8,128)(2,1)S(1)} %collective-permute-done.127), channel_id=1, source_target_pairs={{0,2},{2,4},{4,6},{6,8},{8,10},{10,12},{12,14},{14,16},{16,18},{18... | collective-permute-start | bytes 24584 | tf_op jit(solution)/shard_map/ppermute | solution.py:33
  512.9 13.2 %collective-permute-start.120 = (bf16[32,1,128]{2,0,1:T(8,128)(2,1)}, bf16[32,1,128]{2,0,1:T(8,128)(2,1)S(1)}, u32[]{:S(2)}, u32[]{:S(2)}) collective-permute-start(bf16[32,1,128]{2,0,1:T(8,128)(2,1)} %slice.404), channel_id=1, source_target_pairs={{2,0},{4,2},{6,4},{8,6},{10,8},{12,10},{14,12},{16,14},{18,16},{20... | collective-permute-start | bytes 24584 | tf_op jit(solution)/shard_map/ppermute | solution.py:13
  523.4 7.5 %collective-permute-start.119 = (bf16[32,1,128]{2,0,1:T(8,128)(2,1)}, bf16[32,1,128]{2,0,1:T(8,128)(2,1)S(1)}, u32[]{:S(2)}, u32[]{:S(2)}) collective-permute-start(bf16[32,1,128]{2,0,1:T(8,128)(2,1)} %get-tuple-element.106), channel_id=1, source_target_pairs={{0,2},{2,4},{4,6},{6,8},{8,10},{10,12},{12,14},{14,16},{16,18},{18... | collective-permute-start | bytes 24584 | tf_op jit(solution)/shard_map/ppermute | solution.py:13
  (137 other events, 1050.6 us)
